TPU v7x, 128 devices: a whole 4x4x4 slice. The times are simulated.
128 devices in a mesh: prompts: 8 (over y, core), units: 16 (over x, z).
Axes of the slice: x: 4, y: 4, z: 4, core: 2. Of those that a mesh axis runs over, the one named last changes fastest.
Arguments:
- hidden_acts: bfloat16 [32, 2048, 14336], P('prompts', None, 'units'), may hold values from -6 to 6
- out_grads: bfloat16 [32, 2048, 4096], P('prompts', None, 'units'), may hold values from -6 to 6
- proj_in: bfloat16 [14336, 64], P('units'), may hold values from -0.29231698 to 0.29231698
- proj_out: bfloat16 [4096, 64], P('units'), may hold values from -0.09375 to 0.09375
- lengths: int32 [32], P('prompts'), may hold values from 256 to 2048
- val_grads: float32 [512, 4096], P('prompts', 'units'), may hold values from -6 to 6
Outputs:
- scores: float32 [32, 512], P('prompts')
All inputs are finite; a program needn't handle non-finite values.
Results may differ from a plain program's by a relative error of at most 0.0003.
Values sent between devices are 32-bit elements; how exact they have to be, the bound alone decides.
No kernel may reach another device: no remote copies, remote signals or barrier semaphores. Data moves between devices by JAX's collectives and lax.ppermute only.
A program may use at most 128 MiB of HBM per device.

v0:
```python
import jax
import jax.numpy as jnp
from jax import lax
from jax.sharding import PartitionSpec as P


def project_rows(flat_acts, flat_grads, proj_in, proj_out):
    inner = jnp.dot(flat_acts, proj_in, preferred_element_type=jnp.float32)
    outer = jnp.dot(flat_grads, proj_out, preferred_element_type=jnp.float32)
    return jnp.concatenate([inner, outer], axis=1)


def per_device(hidden_acts, out_grads, proj_in, proj_out, lengths, val_grads):
    prompts_here, seq_len, units_here = hidden_acts.shape
    rank = proj_in.shape[1]
    total_rows = prompts_here * seq_len
    flat_acts = hidden_acts.reshape(total_rows, units_here)
    flat_grads = out_grads.reshape(total_rows, out_grads.shape[2])
    highest = lax.Precision.HIGHEST
    partial_rows = project_rows(flat_acts, flat_grads, proj_in, proj_out)
    summed = lax.psum(partial_rows, "units")
    summed = summed.reshape(prompts_here, seq_len, 2 * rank)
    valid = (jnp.arange(seq_len, dtype=jnp.int32)[None, :] < lengths[:, None]).astype(jnp.float32)
    inner = summed[:, :, :rank] * valid[:, :, None]
    outer = summed[:, :, rank:]
    grads = jnp.einsum("pti,ptj->pij", inner, outer, precision=highest).reshape(
        prompts_here, rank * rank
    )
    val_wide = lax.all_gather(val_grads, "units", axis=1, tiled=True)
    val_all = lax.all_gather(val_wide, "prompts", axis=0, tiled=True)
    dots = jnp.einsum("pf,vf->pv", grads, val_all, precision=highest)
    squares = jnp.sum(grads * grads, axis=1)
    return dots / jnp.sqrt(squares + 1e-06)[:, None]


def solution(mesh):
    in_specs = (
        P("prompts", None, "units"),
        P("prompts", None, "units"),
        P("units", None),
        P("units", None),
        P("prompts"),
        P("prompts", "units"),
    )
    out_specs = P("prompts", None)
    return jax.shard_map(
        per_device, mesh=mesh, in_specs=in_specs, out_specs=out_specs, check_vma=False
    )
```

profile of v0, /device:TPU:0, one launch (start us, length us, event | category | flops | bytes accessed | tf_op | source)
XLA Modules:
  0.0 229.2 jit_solution(14639869188029337980)
XLA Ops:
  6.5 0.0 copy-start
  6.5 0.0 all-gather.3.cloned.1.call-start
  6.5 0.7 all-gather.3.cloned.1.call-update
  7.3 0.0 all-reduce.2.cloned.1.call-start
  7.3 3.6 %fusion.5 = f32[8192,64]{0,1:T(8,128)S(1)} fusion(bf16[8192,256]{1,0:T(8,128)(2,1)} %bitcast.15, bf16[256,64]{0,1:T(8,128)(2,1)} %param.9), kind=kOutput, calls=%fused_computation.12 | convolution fusion | flops 268435456 | bytes 6324224 | tf_op jit(solution)/shard_map/dot_general | solution.py:9
  10.9 0.0 copy-done
  10.9 9.8 %fusion.4 = f32[8192,64]{0,1:T(8,128)S(1)} fusion(bf16[8192,896]{1,0:T(8,128)(2,1)} %bitcast.12, bf16[896,64]{0,1:T(8,128)(2,1)S(1)} %copy-done), kind=kOutput, calls=%fused_computation.11 | convolution fusion | flops 939524096 | bytes 16891904 | tf_op jit(solution)/shard_map/dot_general | solution.py:8
  20.6 0.4 pad_maximum_fusion
  21.0 2.4 %copy.10 = f32[16,4,8,2048]{3,2,0,1:T(8,128)} copy(f32[16,4,8,2048]{3,2,1,0:T(8,128)S(1)} %bitcast.14) | data formatting | bytes 8388608 | tf_op jit(solution)/shard_map/reshape | solution.py:22
  23.5 0.0 copy-start.1
  23.5 0.0 all-reduce.2.cloned.1.call-update
  23.5 0.0 all-gather.5.cloned.1.call-start
  23.5 31.9 %all-gather.3.cloned.1.call-done = f32[64,4096]{1,0:T(8,128)} async-done(((f32[64,256]{1,0:T(8,128)}), f32[64,4096]{1,0:T(8,128)}) %all-gather.3.cloned.1.call-update) | async-done | bytes 1048592 | tf_op jit(solution)/shard_map/all_gather | solution.py:29
  55.5 0.0 all-gather.5.cloned.1.call-update
  55.5 0.0 copy-done.1
  55.5 0.1 fusion.3
  55.6 106.1 %all-reduce.2.cloned.1.call-done = f32[4,2048,128]{1,2,0:T(8,128)} async-done(((f32[4,2048,128]{1,2,0:T(8,128)}), f32[4,2048,128]{1,2,0:T(8,128)}) %all-reduce.2.cloned.1.call-update) | async-done | bytes 4194320 | tf_op jit(solution)/shard_map/psum | solution.py:21
  161.7 4.4 %multiply_reduce_fusion = (f32[4]{0:T(128)S(1)}, f32[4,64,64]{2,1,0:T(8,128)S(1)}) fusion(f32[4,2048,128]{1,2,0:T(8,128)} %all-reduce.2.cloned.1.call-done, f32[4,2048]{1,0:T(4,128)S(1)} %fusion.3), kind=kOutput, calls=%fused_computation.7 | convolution fusion | flops 403210240 | bytes 4292624 | tf_op jit(solution)/shard_map/pti,ptj->pij/dot_general | solution.py:26
  166.1 0.1 reshape.41
  166.2 46.6 %all-gather.5.cloned.1.call-done = f32[512,4096]{1,0:T(8,128)} async-done(((f32[64,4096]{1,0:T(8,128)}), f32[512,4096]{1,0:T(8,128)}) %all-gather.5.cloned.1.call-update) | async-done | bytes 8388624 | tf_op jit(solution)/shard_map/all_gather | solution.py:30
  212.8 9.8 %convolution_divide_fusion = f32[4,512]{1,0:T(4,128)} fusion(f32[4,4096]{1,0:T(4,128)S(1)} %reshape.41, f32[512,4096]{1,0:T(8,128)} %all-gather.5.cloned.1.call-done, f32[4]{0:T(128)S(1)} %add_sqrt_fusion), kind=kOutput, calls=%fused_computation.5 | convolution fusion | flops 100665344 | bytes 8462352 | tf_op jit(solution)/shard_map/pf,vf->pv/dot_general | solution.py:31
  (1 shorter events, 0.0 us)
Async XLA Ops:
  6.5 4.3 %copy-start = (bf16[896,64]{0,1:T(8,128)(2,1)S(1)}, bf16[896,64]{0,1:T(8,128)(2,1)}, u32[]{:S(2)}) copy-start(bf16[896,64]{0,1:T(8,128)(2,1)} %param.8) | copy-start | bytes 344068
  6.5 48.9 %all-gather.3.cloned.1.call-start = ((), (), s32[]{:S(2)}) async-start(), calls=%async_computation.1 | async-start | bytes 1114112 | tf_op jit(solution)/shard_map/all_gather | solution.py:29
  7.3 154.4 %all-reduce.2.cloned.1.call-start = ((), (), s32[]{:S(2)}) async-start(), calls=%async_computation | async-start | bytes 8388608 | tf_op jit(solution)/shard_map/psum | solution.py:21
  23.5 32.0 %copy-start.1 = (s32[4]{0:T(128)S(1)}, s32[4]{0:T(128)}, u32[]{:S(2)}) copy-start(s32[4]{0:T(128)} %param.10) | copy-start | bytes 52
  23.5 189.3 %all-gather.5.cloned.1.call-start = ((), (), s32[]{:S(2)}) async-start(), calls=%async_computation.2 | async-start | bytes 9437184 | tf_op jit(solution)/shard_map/all_gather | solution.py:30
Sparse Core Ops, SparseCore 0:
  9.5 45.9 all-gather.2
  58.8 102.8 all-reduce.1
  163.4 49.3 all-gather.4
where the time goes:
time: 230 us; the launch traced here: 229 us
  waiting for transfers between devices  185 us (80%)
  matrix products  27.5 us (12%)
  between operations  13.1 us (6%)
  local copies, waits for them, and re-layouts  2.56 us (1%)
    psum x1, waiting for transfers between devices, per_device(): summed = lax.psum(partial_rows, 'units')  106 us
    all_gather x1, waiting for transfers between devices, per_device(): val_all = lax.all_gather(val_wide, 'prompts', axis=0, tiled=True)  46.6 us
    all_gather x1, waiting for transfers between devices, per_device(): val_wide = lax.all_gather(val_grads, 'units', axis=1, tiled=True)  31.9 us
    dot_general x1, matrix products, per_device(): dots = jnp.einsum('pf,vf->pv', grads, val_all, precision=highest)  9.8 us
    dot_general x1, matrix products, project_rows(): inner = jnp.dot(flat_acts, proj_in, preferred_element_type=jnp.float32)  9.75 us
  transfers between devices with their start and end apart: 3, of which 3 were waited for; matrix products, arithmetic and copies ran while one was open for 9% of the time, Pallas kernels for 0%

commit v1 on v0

v1 whole, which is shorter than its diff:
```python
import jax
import jax.numpy as jnp
from jax import lax
from jax.experimental import pallas as pl
from jax.experimental.pallas import tpu as pltpu
from jax.sharding import PartitionSpec as P

SIDE = 4
PIECES = 2 * SIDE * SIDE
SLOTS = 2048
GROUP = 4
BLOCK_SIZES = (160, 192, 224, 256)


def blocks_of(scal, p, tb):
    return (scal[p] + (tb - 1)) // tb


def block_info(scal, tb, m):
    second = blocks_of(scal, 0, tb)
    third = second + blocks_of(scal, 1, tb)
    fourth = third + blocks_of(scal, 2, tb)
    end = fourth + blocks_of(scal, 3, tb)
    prompt = (m >= second).astype(jnp.int32) + (m >= third).astype(jnp.int32) + (m >= fourth).astype(jnp.int32)
    first = jnp.where(m >= fourth, fourth, jnp.where(m >= third, third, jnp.where(m >= second, second, 0)))
    token = (m - first) * tb
    inside = m < end
    token = jnp.where(inside, token, 0)
    start = jnp.minimum(token, SLOTS - tb)
    high = jnp.where(inside, scal[prompt] - start, 0)
    return prompt, pl.multiple_of(start, 16), token - start, high


def packed_index(scal, h, j, k):
    x, z = scal[4], scal[5]
    major = jnp.where(h == 0, x, z)
    minor = jnp.where(h == 0, z, x)
    return h * (SIDE * SIDE) + ((major + j) & 3) * SIDE + ((minor + k) & 3)


def plan_kernel(lengths, place, out):
    for p in range(4):
        out[p] = lengths[p]
    out[4] = place[0] >> 2
    out[5] = place[0] & 3
    branch = 0
    for tb in BLOCK_SIZES[:-1]:
        blocks = sum(blocks_of(lengths, p, tb) for p in range(4))
        branch = branch + (blocks > PIECES).astype(jnp.int32)
    out[6] = branch
    out[7] = 0


def project_kernel(tb, steps, scal, acts, grads, w_in, w_out, *refs):
    count = 2 * len(steps)
    outs = refs[:count]
    buf, w_buf, result, bounds, a_sem, g_sem, w_sem, r_sem = refs[count:]
    units = acts.shape[2]
    w_buf[...] = jnp.zeros_like(w_buf)
    weights = [
        pltpu.make_async_copy(w_in, w_buf.at[:64, :units], w_sem.at[0]),
        pltpu.make_async_copy(w_out, w_buf.at[64:, units:], w_sem.at[1]),
    ]
    for copy in weights:
        copy.start()

    def pair(n, k, prompt, start):
        rows = pl.ds(pl.multiple_of(k * tb, 16), tb)
        return (
            pltpu.make_async_copy(acts.at[prompt, pl.ds(start, tb)], buf.at[n, rows, :units], a_sem.at[n]),
            pltpu.make_async_copy(grads.at[prompt, pl.ds(start, tb)], buf.at[n, rows, units:], g_sem.at[n]),
        )

    def fetch(i, _):
        n, k = i >> 2, i & 3
        j = steps[-1]
        for place, step in enumerate(steps[:-1]):
            j = jnp.where(n >> 1 == place, step, j)
        prompt, start, low, high = block_info(scal, tb, packed_index(scal, n & 1, j, k))
        bounds[i, 0] = low
        bounds[i, 1] = high
        for copy in pair(n, k, prompt, start):
            copy.start()
        return 0

    lax.fori_loop(0, count * SIDE, fetch, 0)
    for copy in weights:
        copy.wait()
    row = lax.broadcasted_iota(jnp.int32, (tb, 128), 0)

    def hand_over(n, act):
        for q in range(count):
            @pl.when(n == q)
            def _():
                act(pltpu.make_async_copy(result.at[q & 1], outs[q], r_sem.at[q & 1]))

    def compute(n, _):
        for k in range(SIDE):
            for copy in pair(n, k, 0, 0):
                copy.wait()
        hand_over(n - 2, lambda copy: copy.wait())
        for c in range(SIDE // GROUP):
            both = lax.dot_general(
                buf[n, c * GROUP * tb : (c + 1) * GROUP * tb], w_buf[...], (((1,), (1,)), ((), ())),
                preferred_element_type=jnp.float32,
            )
            for k in range(GROUP):
                at = c * GROUP + k
                keep = (row >= bounds[n * SIDE + at, 0]) & (row < bounds[n * SIDE + at, 1])
                result[n & 1, at] = jnp.where(keep, both[k * tb : (k + 1) * tb], 0.0)
        hand_over(n, lambda copy: copy.start())
        return 0

    lax.fori_loop(0, count, compute, 0)
    for q in range(count - 2, count):
        pltpu.make_async_copy(result.at[q & 1], outs[q], r_sem.at[q & 1]).wait()


def project(tb, steps, scal, acts, grads, w_in, w_out):
    units, width = acts.shape[2], grads.shape[2]
    count = 2 * len(steps)
    rows = count * SIDE * tb
    return pl.pallas_call(
        lambda *refs: project_kernel(tb, steps, *refs),
        in_specs=[pl.BlockSpec(memory_space=pltpu.SMEM)] + [pl.BlockSpec(memory_space=pl.ANY)] * 4,
        out_specs=[pl.BlockSpec(memory_space=pltpu.VMEM)] * count,
        out_shape=[jax.ShapeDtypeStruct((SIDE, tb, 128), jnp.float32)] * count,
        scratch_shapes=[
            pltpu.VMEM((count, SIDE * tb, units + width), jnp.bfloat16),
            pltpu.VMEM((128, units + width), jnp.bfloat16),
            pltpu.VMEM((2, SIDE, tb, 128), jnp.float32),
            pltpu.SMEM((count * SIDE, 2), jnp.int32),
            pltpu.SemaphoreType.DMA((count,)),
            pltpu.SemaphoreType.DMA((count,)),
            pltpu.SemaphoreType.DMA((2,)),
            pltpu.SemaphoreType.DMA((2,)),
        ],
        compiler_params=pltpu.CompilerParams(vmem_limit_bytes=36 * 1024 * 1024),
        cost_estimate=pl.CostEstimate(
            flops=2 * rows * (units + width) * 256,
            bytes_accessed=rows * ((units + width) * 2 + 512),
            transcendentals=0,
        ),
    )(scal, acts, grads, w_in, w_out)


def outer_kernel(tb, scal, *refs):
    out = refs[-1]
    row = lax.broadcasted_iota(jnp.int32, (64, 64), 0)
    col = lax.broadcasted_iota(jnp.int32, (64, 64), 1)
    order = ((row & 15) * 4 + (row >> 4) == col).astype(jnp.float32)
    each, owner = [], []
    for h in range(2):
        a, b, c, d = (ref[...] for ref in refs[4 * h : 4 * h + 4])
        rows = (a + b) + (c + d)
        product = lax.dot_general(
            rows[:, :64], rows[:, 64:], (((0,), (0,)), ((), ())),
            precision=lax.Precision.HIGHEST, preferred_element_type=jnp.float32,
        )
        each.append(jnp.dot(order, product, precision=lax.Precision.HIGHEST, preferred_element_type=jnp.float32))
        owner.append(block_info(scal, tb, packed_index(scal, h, 0, 0))[0])
    for p in range(4):
        total = jnp.where(owner[0] == p, each[0], 0.0) + jnp.where(owner[1] == p, each[1], 0.0)
        for i in range(4):
            out[:, p, i * 64 : (i + 1) * 64] = total[i * 16 : (i + 1) * 16]


def along(axis, step):
    pairs = []
    for x in range(SIDE):
        for z in range(SIDE):
            if axis == "x":
                pairs.append((x * SIDE + z, (x + step) % SIDE * SIDE + z))
            else:
                pairs.append((x * SIDE + z, x * SIDE + (z + step) % SIDE))
    return pairs


def send(value, axis, step):
    return lax.ppermute(value, "units", along(axis, step))


def reduce_blocks(tb, scal, acts, grads, w_in, w_out):
    x2, z2 = project(tb, (2,), scal, acts, grads, w_in, w_out)
    got_x = [send(x2, "x", 2)]
    got_z = [send(z2, "z", 2)]
    x1, z1, x3, z3, x0, z0 = project(tb, (1, 3, 0), scal, acts, grads, w_in, w_out)
    got_x += [send(x1, "x", 1), send(x3, "x", 3)]
    got_z += [send(z1, "z", 1), send(z3, "z", 3)]
    total_x = x0 + sum(got_x)
    total_z = z0 + sum(got_z)
    final = []
    for total, axis in ((total_x, "z"), (total_z, "x")):
        final.append(total[0])
        final += [send(total[k], axis, k) for k in (2, 1, 3)]
    return pl.pallas_call(
        lambda *refs: outer_kernel(tb, *refs),
        in_specs=[pl.BlockSpec(memory_space=pltpu.SMEM)] + [pl.BlockSpec(memory_space=pltpu.VMEM)] * 8,
        out_specs=pl.BlockSpec(memory_space=pltpu.VMEM),
        out_shape=jax.ShapeDtypeStruct((16, 4, 256), jnp.float32),
    )(scal, *final)


def dots_kernel(received, pair_0, pair_1, pair_2, pair_3, out):
    grads = jnp.sum(received[...], axis=0)
    squares = jnp.sum(grads * grads, axis=1, keepdims=True)
    parts = []
    for pair in (pair_0, pair_1, pair_2, pair_3):
        parts.append(lax.dot_general(
            grads, pair[...], (((1,), (1,)), ((), ())),
            precision=lax.Precision.HIGHEST, preferred_element_type=jnp.float32,
        ))
    parts.append(jnp.broadcast_to(squares, (4, 128)))
    packed = jnp.concatenate(parts, axis=1)
    out[...] = jnp.broadcast_to(packed[None], out.shape)


def scores_kernel(group, received, out):
    sums = jnp.sum(received[...], axis=0)
    scale = jnp.sqrt(sums[:, 512:640] + 1e-06)
    y, core = group[0] >> 1, group[0] & 1
    for n in range(4):
        part = pltpu.roll(sums[:, n * 128 : (n + 1) * 128], core * 64, 1) / scale
        out[:, pl.ds(pl.multiple_of(((y - n) & 3) * 128, 128), 128)] = part


def per_device(hidden_acts, out_grads, proj_in, proj_out, lengths, val_grads):
    place = lax.axis_index("units").astype(jnp.int32).reshape(1)
    group = lax.axis_index("prompts").astype(jnp.int32).reshape(1)
    smem = pl.BlockSpec(memory_space=pltpu.SMEM)
    vmem = pl.BlockSpec(memory_space=pltpu.VMEM)
    other = lax.ppermute(val_grads, "prompts", [(n, n ^ 1) for n in range(8)])
    scal = pl.pallas_call(
        plan_kernel,
        in_specs=[smem] * 2,
        out_specs=smem,
        out_shape=jax.ShapeDtypeStruct((8,), jnp.int32),
    )(lengths, place)
    shards = lax.switch(
        scal[6],
        [lambda *ops, tb=tb: reduce_blocks(tb, *ops) for tb in BLOCK_SIZES],
        scal, hidden_acts, out_grads, proj_in.T, proj_out.T,
    )
    pairs = [jnp.concatenate([val_grads, other])]
    for step in (1, 3, 2):
        hops = [(2 * y + c, 2 * ((y + step) % 4) + c) for y in range(4) for c in range(2)]
        pairs.append(lax.ppermute(pairs[0], "prompts", hops))
    pairs = [pairs[0], pairs[1], pairs[3], pairs[2]]
    received = lax.all_to_all(shards, "units", 0, 0, tiled=True)
    packed = pl.pallas_call(
        dots_kernel,
        in_specs=[vmem] * 5,
        out_specs=vmem,
        out_shape=jax.ShapeDtypeStruct((16, 4, 640), jnp.float32),
    )(received, *pairs)
    return pl.pallas_call(
        scores_kernel,
        in_specs=[smem, vmem],
        out_specs=vmem,
        out_shape=jax.ShapeDtypeStruct((4, 512), jnp.float32),
    )(group, lax.all_to_all(packed, "units", 0, 0, tiled=True))


def solution(mesh):
    in_specs = (
        P("prompts", None, "units"),
        P("prompts", None, "units"),
        P("units", None),
        P("units", None),
        P("prompts"),
        P("prompts", "units"),
    )
    return jax.shard_map(
        per_device, mesh=mesh, in_specs=in_specs, out_specs=P("prompts", None), check_vma=False
    )
```

time: 230 us -> 93.4 us (0.41)
  waiting for transfers between devices: 185 us -> 18.6 us
  starting transfers between devices: 0.08 us -> 34.6 us
  matrix products: 27.5 us -> 0 us
  Pallas kernels: 0 us -> 19.5 us
  blocking collectives: 0 us -> 12.9 us
  between operations: 13.1 us -> 0.73 us
  local copies, waits for them, and re-layouts: 2.56 us -> 5.68 us
    psum x1 -> x0, waiting for transfers between devices: 106 us -> none  [per_device(): summed = lax.psum(partial_rows, 'units')]
    all_gather x2 -> x0, waiting for transfers between devices: 78.5 us -> none  [the longest x1 46.6 us: per_device(): val_all = lax.all_gather(val_wide, 'prompts', axis=0, tiled=True)]
    ppermute x0 -> x16, starting transfers between devices: none -> 31.1 us  [the longest x12 24.8 us: send(): return lax.ppermute(value, 'units', along(axis, step))]
    dot_general x4 -> x0, matrix products: 27.5 us -> none  [the longest x1 9.8 us: per_device(): dots = jnp.einsum('pf,vf->pv', grads, val_all, precision=highest)]
    pallas_call x0 -> x6, Pallas kernels: none -> 19.5 us  [the longest x2 11.9 us: project(): pl.pallas_call(lambda *refs: project_kernel(tb, steps, *refs), in_specs=[...]
    all_to_all x0 -> x1, blocking collectives: none -> 12.9 us  [per_device(): received = lax.all_to_all(shards, 'units', 0, 0, tiled=True)]
    ppermute x0 -> x16, waiting for transfers between devices: none -> 10.7 us  [the longest x12 10.1 us: send(): return lax.ppermute(value, 'units', along(axis, step))]
    all_to_all x0 -> x1, waiting for transfers between devices: none -> 7.9 us  [per_device(): lax.all_to_all(packed, 'units', 0, 0, tiled=True)]
  transfers between devices with their start and end apart: 3 -> 17, of which waited for: 3 -> 7; matrix products, arithmetic and copies ran while one was open for 9% -> 3% of each run, Pallas kernels for 0% -> 9%
where the time goes in v1:
time: 93.4 us; the launch traced here: 92.5 us
  starting transfers between devices  34.6 us (37%)
  Pallas kernels  19.5 us (21%)
  waiting for transfers between devices  18.6 us (20%)
  blocking collectives  12.9 us (14%)
  local copies, waits for them, and re-layouts  5.68 us (6%)
    ppermute x12, starting transfers between devices, send(): return lax.ppermute(value, 'units', along(axis, step))  24.8 us
    all_to_all x1, blocking collectives, per_device(): received = lax.all_to_all(shards, 'units', 0, 0, tiled=True)  12.9 us
    pallas_call x2, Pallas kernels, project(): pl.pallas_call(lambda *refs: project_kernel(tb, steps, *refs), in_specs=[...  11.9 us
    ppermute x12, waiting for transfers between devices, send(): return lax.ppermute(value, 'units', along(axis, step))  10.1 us
    all_to_all x1, waiting for transfers between devices, per_device(): lax.all_to_all(packed, 'units', 0, 0, tiled=True)  7.9 us
    ppermute x3, starting transfers between devices, per_device(): pairs.append(lax.ppermute(pairs[0], 'prompts', hops))  6.17 us
    all_to_all x1, starting transfers between devices, per_device(): lax.all_to_all(packed, 'units', 0, 0, tiled=True)  3.52 us
    unnamed x11, local copies, waits for them, and re-layouts  2.84 us
  transfers between devices with their start and end apart: 17, of which 7 were waited for; matrix products, arithmetic and copies ran while one was open for 3% of the time, Pallas kernels for 9%

profile of v1, /device:TPU:0, one launch (start us, length us, event | category | flops | bytes accessed | tf_op | source)
XLA Modules:
  0.0 92.5 jit_solution(15682241746358677999)
XLA Ops:
  0.0 1.3 %shard_map.64 = s32[8]{0:T(128)S(1)} custom-call(s32[4]{0:T(128)} %lengths.1, s32[1]{0:T(128)} %bitcast.33.place), custom_call_target="tpu_custom_call" | custom-call | tf_op jit(solution)/shard_map/pallas_call | solution.py:233
  1.3 0.6 slice.99
  2.6 51.9 %conditional.1 = (f32[16,4,256]{2,1,0:T(4,128)S(1)}) conditional(s32[]{:T(128)} %bitcast.34, (s32[8]{0:T(128)S(1)}, bf16[4,2048,896]{2,1,0:T(8,128)(2,1)}, bf16[4,2048,256]{2,1,0:T(8,128)(2,1)}, bf16[64,896]{1,0:T(8,128)(2,1)}, bf16[64,256]{1,0:T(8,128)(2,1)}) %tuple.50, (s32[8]{0:T(128)S(1)}, ...), branch_computations={%region_0.0_spmd, %region_1.0_spmd, %region_2.0_spmd, %region_3.0_... | conditional | flops 4832624640 | bytes 125371136 | solution.py:239
  2.6 0.0 copy-start.1
  2.6 0.0 copy-start.5
  2.6 0.0 copy-start.9
  2.6 0.0 copy-start.13
  2.6 4.0 %branch_1_fun.4 = (f32[4,192,128]{2,1,0:T(8,128)S(1)}, f32[4,192,128]{2,1,0:T(8,128)S(1)}) custom-call(s32[8]{0:T(128)S(1)} %get-tuple-element.63.refs_0_, bf16[4,2048,896]{2,1,0:T(8,128)(2,1)} %get-tuple-element.64.refs_1_, bf16[4,2048,256]{2,1,0:T(8,128)(2,1)} %get-tuple-element.65.refs_2_, bf16[64,896]{1,0:T(8,128)(2,1)} %get-tuple-element.66.refs_3_, ...), custom_call_target="tpu_custom_call" | custom-call | flops 905969664 | bytes 4325376 | tf_op jit(solution)/shard_map/cond/branch_1_fun/pallas_call | solution.py:123
  6.7 3.2 %collective-permute-start.12 = (f32[4,192,128]{2,1,0:T(8,128)S(1)}, f32[4,192,128]{2,1,0:T(8,128)S(1)}, u32[]{:S(2)}, u32[]{:S(2)}) collective-permute-start(f32[4,192,128]{2,1,0:T(8,128)S(1)} %get-tuple-element.69), channel_id=1, source_target_pairs={{0,8},{1,9},{2,10},{3,11},{4,12},{5,13},{6,14},{7,15},{8,0},{9,1},... | collective-permute-start | bytes 1179656 | tf_op jit(solution)/shard_map/cond/branch_1_fun/ppermute | solution.py:180
  9.9 0.2 copy-done.5
  10.1 7.9 %branch_1_fun.3 = (f32[4,192,128]{2,1,0:T(8,128)S(1)}, f32[4,192,128]{2,1,0:T(8,128)S(1)}, f32[4,192,128]{2,1,0:T(8,128)S(1)}, f32[4,192,128]{2,1,0:T(8,128)S(1)...) custom-call(s32[8]{0:T(128)S(1)} %get-tuple-element.63.refs_0_, bf16[4,2048,896]{2,1,0:T(8,128)(2,1)S(1)} %copy-done.1, ...), custom_call_target="tpu_custom_call" | custom-call | flops 2717908992 | bytes 12976128 | tf_op jit(solution)/shard_map/cond/branch_1_fun/pallas_call | solution.py:123
  18.0 1.6 %collective-permute-start.13 = (f32[4,192,128]{2,1,0:T(8,128)S(1)}, f32[4,192,128]{2,1,0:T(8,128)S(1)}, u32[]{:S(2)}, u32[]{:S(2)}) collective-permute-start(f32[4,192,128]{2,1,0:T(8,128)S(1)} %get-tuple-element.70), channel_id=1, source_target_pairs={{0,4},{1,5},{2,6},{3,7},{4,8},{5,9},{6,10},{7,11},{8,12},{9,13},{1... | collective-permute-start | bytes 1179656 | tf_op jit(solution)/shard_map/cond/branch_1_fun/ppermute | solution.py:180
  19.6 1.7 %collective-permute-start.14 = (f32[4,192,128]{2,1,0:T(8,128)S(1)}, f32[4,192,128]{2,1,0:T(8,128)S(1)}, u32[]{:S(2)}, u32[]{:S(2)}) collective-permute-start(f32[4,192,128]{2,1,0:T(8,128)S(1)} %get-tuple-element.71), channel_id=1, source_target_pairs={{0,12},{1,13},{2,14},{3,15},{4,0},{5,1},{6,2},{7,3},{8,4},{9,5},{1... | collective-permute-start | bytes 1179656 | tf_op jit(solution)/shard_map/cond/branch_1_fun/ppermute | solution.py:180
  21.3 4.0 %collective-permute-start.18 = (f32[4,192,128]{2,1,0:T(8,128)S(1)}, f32[4,192,128]{2,1,0:T(8,128)S(1)}, u32[]{:S(2)}, u32[]{:S(2)}) collective-permute-start(f32[4,192,128]{2,1,0:T(8,128)S(1)} %get-tuple-element.73), channel_id=1, source_target_pairs={{0,2},{1,3},{2,0},{3,1},{4,6},{5,7},{6,4},{7,5},{8,10},{9,11},{10,... | collective-permute-start | bytes 1179656 | tf_op jit(solution)/shard_map/cond/branch_1_fun/ppermute | solution.py:180
  25.3 1.0 %collective-permute-start.19 = (f32[4,192,128]{2,1,0:T(8,128)S(1)}, f32[4,192,128]{2,1,0:T(8,128)S(1)}, u32[]{:S(2)}, u32[]{:S(2)}) collective-permute-start(f32[4,192,128]{2,1,0:T(8,128)S(1)} %get-tuple-element.74), channel_id=1, source_target_pairs={{0,1},{1,2},{2,3},{3,0},{4,5},{5,6},{6,7},{7,4},{8,9},{9,10},{10,1... | collective-permute-start | bytes 1179656 | tf_op jit(solution)/shard_map/cond/branch_1_fun/ppermute | solution.py:180
  26.3 2.2 %collective-permute-start.20 = (f32[4,192,128]{2,1,0:T(8,128)S(1)}, f32[4,192,128]{2,1,0:T(8,128)S(1)}, u32[]{:S(2)}, u32[]{:S(2)}) collective-permute-start(f32[4,192,128]{2,1,0:T(8,128)S(1)} %get-tuple-element.75), channel_id=1, source_target_pairs={{0,3},{1,0},{2,1},{3,2},{4,7},{5,4},{6,5},{7,6},{8,11},{9,8},{10,9... | collective-permute-start | bytes 1179656 | tf_op jit(solution)/shard_map/cond/branch_1_fun/ppermute | solution.py:180
  28.5 0.1 add_add_fusion.3
  28.6 0.7 slice_bitcast_fusion.12
  29.3 3.8 %collective-permute-start.17 = (f32[192,128]{1,0:T(8,128)S(1)}, f32[192,128]{1,0:T(8,128)S(1)}, u32[]{:S(2)}, u32[]{:S(2)}) collective-permute-start(f32[192,128]{1,0:T(8,128)S(1)} %get-tuple-element.114), channel_id=1, source_target_pairs={{0,3},{1,0},{2,1},{3,2},{4,7},{5,4},{6,5},{7,6},{8,11},{9,8},{10,9... | collective-permute-start | bytes 294920 | tf_op jit(solution)/shard_map/cond/branch_1_fun/ppermute | solution.py:180
  33.0 2.3 %collective-permute-done.18 = f32[4,192,128]{2,1,0:T(8,128)S(1)} collective-permute-done((f32[4,192,128]{2,1,0:T(8,128)S(1)}, f32[4,192,128]{2,1,0:T(8,128)S(1)}, u32[]{:S(2)}, u32[]{:S(2)}) %collective-permute-start.18) | collective-permute-done | bytes 393248 | tf_op jit(solution)/shard_map/cond/branch_1_fun/ppermute | solution.py:180
  35.3 3.5 %collective-permute-start.15 = (f32[192,128]{1,0:T(8,128)S(1)}, f32[192,128]{1,0:T(8,128)S(1)}, u32[]{:S(2)}, u32[]{:S(2)}) collective-permute-start(f32[192,128]{1,0:T(8,128)S(1)} %get-tuple-element.116), channel_id=1, source_target_pairs={{0,2},{1,3},{2,0},{3,1},{4,6},{5,7},{6,4},{7,5},{8,10},{9,11},{10,... | collective-permute-start | bytes 294920 | tf_op jit(solution)/shard_map/cond/branch_1_fun/ppermute | solution.py:180
  38.8 2.5 %collective-permute-done.19 = f32[4,192,128]{2,1,0:T(8,128)S(1)} collective-permute-done((f32[4,192,128]{2,1,0:T(8,128)S(1)}, f32[4,192,128]{2,1,0:T(8,128)S(1)}, u32[]{:S(2)}, u32[]{:S(2)}) %collective-permute-start.19) | collective-permute-done | bytes 393248 | tf_op jit(solution)/shard_map/cond/branch_1_fun/ppermute | solution.py:180
  41.3 0.8 collective-permute-done.20
  42.1 0.1 add_add_fusion.2
  42.2 0.7 slice_bitcast_fusion.8
  42.8 1.6 %collective-permute-start.23 = (f32[192,128]{1,0:T(8,128)S(1)}, f32[192,128]{1,0:T(8,128)S(1)}, u32[]{:S(2)}, u32[]{:S(2)}) collective-permute-start(f32[192,128]{1,0:T(8,128)S(1)} %get-tuple-element.110), channel_id=1, source_target_pairs={{0,12},{1,13},{2,14},{3,15},{4,0},{5,1},{6,2},{7,3},{8,4},{9,5},{1... | collective-permute-start | bytes 294920 | tf_op jit(solution)/shard_map/cond/branch_1_fun/ppermute | solution.py:180
  44.4 0.5 collective-permute-start.22
  44.9 1.8 %collective-permute-start.21 = (f32[192,128]{1,0:T(8,128)S(1)}, f32[192,128]{1,0:T(8,128)S(1)}, u32[]{:S(2)}, u32[]{:S(2)}) collective-permute-start(f32[192,128]{1,0:T(8,128)S(1)} %get-tuple-element.112), channel_id=1, source_target_pairs={{0,8},{1,9},{2,10},{3,11},{4,12},{5,13},{6,14},{7,15},{8,0},{9,1},... | collective-permute-start | bytes 294920 | tf_op jit(solution)/shard_map/cond/branch_1_fun/ppermute | solution.py:180
  46.7 0.7 collective-permute-done.23.refs_8_
  47.5 3.8 %collective-permute-done.22.refs_7_ = f32[192,128]{1,0:T(8,128)S(1)} collective-permute-done((f32[192,128]{1,0:T(8,128)S(1)}, f32[192,128]{1,0:T(8,128)S(1)}, u32[]{:S(2)}, u32[]{:S(2)}) %collective-permute-start.22) | collective-permute-done | bytes 98336 | tf_op jit(solution)/shard_map/cond/branch_1_fun/ppermute | solution.py:180
  51.3 0.6 copy-done.37
  51.9 0.0 copy-done.38
  52.0 2.3 %branch_1_fun.5 = f32[16,4,256]{2,1,0:T(4,128)S(1)} custom-call(s32[8]{0:T(128)S(1)} %get-tuple-element.63.refs_0_, f32[192,128]{1,0:T(8,128)} %get-tuple-element.117.refs_1_, f32[192,128]{1,0:T(8,128)} %copy-done.35, f32[192,128]{1,0:T(8,128)} %copy-done.34, f32[192,128]{1,0:T(8,128)} %copy-done.33, f32[192,128]{1,0:T(8,128)} %get-tuple-element.113.refs_5_, ...), custom_call_target="tpu_custom_call" | custom-call | tf_op jit(solution)/shard_map/cond/branch_1_fun/pallas_call | solution.py:196
  54.5 0.1 collective-permute-start.48
  54.6 0.8 constant_dynamic-update-slice_fusion.1
  55.4 0.6 collective-permute-done.48
  56.0 4.8 %collective-permute-start.51 = (f32[128,256]{1,0:T(8,128)S(1)}, f32[128,256]{1,0:T(8,128)S(1)}, u32[]{:S(2)}, u32[]{:S(2)}) collective-permute-start(f32[128,256]{1,0:T(8,128)S(1)} %constant_dynamic-update-slice_fusion.pair_0), channel_id=1, source_target_pairs={{0,96},{16,112},{32,0},{48,16},{64,32},{80,48},{96,64},{112,80},{1... | collective-permute-start | bytes 393224 | tf_op jit(solution)/shard_map/ppermute | solution.py:247
  60.8 0.4 collective-permute-start.50
  61.2 1.0 %collective-permute-start.49 = (f32[128,256]{1,0:T(8,128)S(1)}, f32[128,256]{1,0:T(8,128)S(1)}, u32[]{:S(2)}, u32[]{:S(2)}) collective-permute-start(f32[128,256]{1,0:T(8,128)S(1)} %constant_dynamic-update-slice_fusion.pair_0), channel_id=1, source_target_pairs={{0,32},{16,48},{32,64},{48,80},{64,96},{80,112},{96,0},{112,16},{1... | collective-permute-start | bytes 393224 | tf_op jit(solution)/shard_map/ppermute | solution.py:247
  62.2 12.9 %all_to_all.10.received = f32[16,4,256]{2,1,0:T(4,128)} all-to-all(f32[16,4,256]{2,1,0:T(4,128)S(1)} %get-tuple-element.134), channel_id=1, replica_groups=mesh['prompts'=8,'units'=16] {'units'}, dimensions={0} | all-to-all | bytes 131072 | tf_op jit(solution)/shard_map/all_to_all | solution.py:249
  75.1 0.6 copy-done.18
  75.8 0.1 copy-done.19
  75.8 0.7 copy-done.20
  76.5 2.3 %shard_map.65 = f32[16,4,640]{2,1,0:T(4,128)} custom-call(f32[16,4,256]{2,1,0:T(4,128)} %all_to_all.10.received, f32[128,256]{1,0:T(8,128)} %copy-done.17, f32[128,256]{1,0:T(8,128)} %copy-done.20, f32[128,256]{1,0:T(8,128)} %copy-done.19, f32[128,256]{1,0:T(8,128)} %copy-done.18), custom_call_target="tpu_custom_call" | custom-call | tf_op jit(solution)/shard_map/pallas_call | solution.py:250
  78.8 3.5 %all-to-all-start.1 = ((f32[16,4,640]{2,1,0:T(4,128)}), f32[16,4,640]{2,1,0:T(4,128)S(1)}, u32[]{:S(2)}, u32[]{:S(2)}) async-start(f32[16,4,640]{2,1,0:T(4,128)} %shard_map.65), calls=%async_computation.1 | async-start | bytes 327680 | tf_op jit(solution)/shard_map/all_to_all | solution.py:261
  82.3 7.9 %all-to-all-done.1.received = f32[16,4,640]{2,1,0:T(4,128)S(1)} async-done(((f32[16,4,640]{2,1,0:T(4,128)}), f32[16,4,640]{2,1,0:T(4,128)S(1)}, u32[]{:S(2)}, u32[]{:S(2)}) %all-to-all-start.1) | async-done | bytes 163872 | tf_op jit(solution)/shard_map/all_to_all | solution.py:261
  90.2 0.7 copy-done.16
  90.9 1.6 %shard_map.66 = f32[4,512]{1,0:T(4,128)} custom-call(s32[1]{0:T(128)} %bitcast.32.group, f32[16,4,640]{2,1,0:T(4,128)} %copy-done.16), custom_call_target="tpu_custom_call" | custom-call | tf_op jit(solution)/shard_map/pallas_call | solution.py:256
  (31 shorter events, 0.1 us)
Async XLA Ops:
  2.6 7.3 %copy-start.1 = (bf16[4,2048,896]{2,1,0:T(8,128)(2,1)S(1)}, bf16[4,2048,896]{2,1,0:T(8,128)(2,1)}, u32[]{:S(2)}) copy-start(bf16[4,2048,896]{2,1,0:T(8,128)(2,1)} %get-tuple-element.64.refs_1_) | copy-start | bytes 44040196 | tf_op jit(solution)/shard_map/cond
  2.6 7.5 %copy-start.5 = (bf16[4,2048,256]{2,1,0:T(8,128)(2,1)S(1)}, bf16[4,2048,256]{2,1,0:T(8,128)(2,1)}, u32[]{:S(2)}) copy-start(bf16[4,2048,256]{2,1,0:T(8,128)(2,1)} %get-tuple-element.65.refs_2_) | copy-start | bytes 12582916 | tf_op jit(solution)/shard_map/cond
  2.6 7.5 %copy-start.9 = (bf16[64,896]{1,0:T(8,128)(2,1)S(1)}, bf16[64,896]{1,0:T(8,128)(2,1)}, u32[]{:S(2)}) copy-start(bf16[64,896]{1,0:T(8,128)(2,1)} %get-tuple-element.66.refs_3_) | copy-start | bytes 344068 | tf_op jit(solution)/shard_map/cond
  2.6 7.5 %copy-start.13 = (bf16[64,256]{1,0:T(8,128)(2,1)S(1)}, bf16[64,256]{1,0:T(8,128)(2,1)}, u32[]{:S(2)}) copy-start(bf16[64,256]{1,0:T(8,128)(2,1)} %get-tuple-element.67.refs_4_) | copy-start | bytes 98308 | tf_op jit(solution)/shard_map/cond
  6.7 19.6 %collective-permute-start.12 = (f32[4,192,128]{2,1,0:T(8,128)S(1)}, f32[4,192,128]{2,1,0:T(8,128)S(1)}, u32[]{:S(2)}, u32[]{:S(2)}) collective-permute-start(f32[4,192,128]{2,1,0:T(8,128)S(1)} %get-tuple-element.69), channel_id=1, source_target_pairs={{0,8},{1,9},{2,10},{3,11},{4,12},{5,13},{6,14},{7,15},{8,0},{9,1},... | collective-permute-start | bytes 1179656 | tf_op jit(solution)/shard_map/cond/branch_1_fun/ppermute | solution.py:180
  18.0 10.5 %collective-permute-start.13 = (f32[4,192,128]{2,1,0:T(8,128)S(1)}, f32[4,192,128]{2,1,0:T(8,128)S(1)}, u32[]{:S(2)}, u32[]{:S(2)}) collective-permute-start(f32[4,192,128]{2,1,0:T(8,128)S(1)} %get-tuple-element.70), channel_id=1, source_target_pairs={{0,4},{1,5},{2,6},{3,7},{4,8},{5,9},{6,10},{7,11},{8,12},{9,13},{1... | collective-permute-start | bytes 1179656 | tf_op jit(solution)/shard_map/cond/branch_1_fun/ppermute | solution.py:180
  19.6 8.9 %collective-permute-start.14 = (f32[4,192,128]{2,1,0:T(8,128)S(1)}, f32[4,192,128]{2,1,0:T(8,128)S(1)}, u32[]{:S(2)}, u32[]{:S(2)}) collective-permute-start(f32[4,192,128]{2,1,0:T(8,128)S(1)} %get-tuple-element.71), channel_id=1, source_target_pairs={{0,12},{1,13},{2,14},{3,15},{4,0},{5,1},{6,2},{7,3},{8,4},{9,5},{1... | collective-permute-start | bytes 1179656 | tf_op jit(solution)/shard_map/cond/branch_1_fun/ppermute | solution.py:180
  21.3 14.0 %collective-permute-start.18 = (f32[4,192,128]{2,1,0:T(8,128)S(1)}, f32[4,192,128]{2,1,0:T(8,128)S(1)}, u32[]{:S(2)}, u32[]{:S(2)}) collective-permute-start(f32[4,192,128]{2,1,0:T(8,128)S(1)} %get-tuple-element.73), channel_id=1, source_target_pairs={{0,2},{1,3},{2,0},{3,1},{4,6},{5,7},{6,4},{7,5},{8,10},{9,11},{10,... | collective-permute-start | bytes 1179656 | tf_op jit(solution)/shard_map/cond/branch_1_fun/ppermute | solution.py:180
  25.3 16.1 %collective-permute-start.19 = (f32[4,192,128]{2,1,0:T(8,128)S(1)}, f32[4,192,128]{2,1,0:T(8,128)S(1)}, u32[]{:S(2)}, u32[]{:S(2)}) collective-permute-start(f32[4,192,128]{2,1,0:T(8,128)S(1)} %get-tuple-element.74), channel_id=1, source_target_pairs={{0,1},{1,2},{2,3},{3,0},{4,5},{5,6},{6,7},{7,4},{8,9},{9,10},{10,1... | collective-permute-start | bytes 1179656 | tf_op jit(solution)/shard_map/cond/branch_1_fun/ppermute | solution.py:180
  26.3 15.8 %collective-permute-start.20 = (f32[4,192,128]{2,1,0:T(8,128)S(1)}, f32[4,192,128]{2,1,0:T(8,128)S(1)}, u32[]{:S(2)}, u32[]{:S(2)}) collective-permute-start(f32[4,192,128]{2,1,0:T(8,128)S(1)} %get-tuple-element.75), channel_id=1, source_target_pairs={{0,3},{1,0},{2,1},{3,2},{4,7},{5,4},{6,5},{7,6},{8,11},{9,8},{10,9... | collective-permute-start | bytes 1179656 | tf_op jit(solution)/shard_map/cond/branch_1_fun/ppermute | solution.py:180
  29.3 15.6 %collective-permute-start.17 = (f32[192,128]{1,0:T(8,128)S(1)}, f32[192,128]{1,0:T(8,128)S(1)}, u32[]{:S(2)}, u32[]{:S(2)}) collective-permute-start(f32[192,128]{1,0:T(8,128)S(1)} %get-tuple-element.114), channel_id=1, source_target_pairs={{0,3},{1,0},{2,1},{3,2},{4,7},{5,4},{6,5},{7,6},{8,11},{9,8},{10,9... | collective-permute-start | bytes 294920 | tf_op jit(solution)/shard_map/cond/branch_1_fun/ppermute | solution.py:180
  33.0 13.7 %collective-permute-start.16 = (f32[192,128]{1,0:T(8,128)S(1)}, f32[192,128]{1,0:T(8,128)S(1)}, u32[]{:S(2)}, u32[]{:S(2)}) collective-permute-start(f32[192,128]{1,0:T(8,128)S(1)} %get-tuple-element.115), channel_id=1, source_target_pairs={{0,1},{1,2},{2,3},{3,0},{4,5},{5,6},{6,7},{7,4},{8,9},{9,10},{10,1... | collective-permute-start | bytes 294920 | tf_op jit(solution)/shard_map/cond/branch_1_fun/ppermute | solution.py:180
  35.3 11.4 %collective-permute-start.15 = (f32[192,128]{1,0:T(8,128)S(1)}, f32[192,128]{1,0:T(8,128)S(1)}, u32[]{:S(2)}, u32[]{:S(2)}) collective-permute-start(f32[192,128]{1,0:T(8,128)S(1)} %get-tuple-element.116), channel_id=1, source_target_pairs={{0,2},{1,3},{2,0},{3,1},{4,6},{5,7},{6,4},{7,5},{8,10},{9,11},{10,... | collective-permute-start | bytes 294920 | tf_op jit(solution)/shard_map/cond/branch_1_fun/ppermute | solution.py:180
  42.8 4.6 %collective-permute-start.23 = (f32[192,128]{1,0:T(8,128)S(1)}, f32[192,128]{1,0:T(8,128)S(1)}, u32[]{:S(2)}, u32[]{:S(2)}) collective-permute-start(f32[192,128]{1,0:T(8,128)S(1)} %get-tuple-element.110), channel_id=1, source_target_pairs={{0,12},{1,13},{2,14},{3,15},{4,0},{5,1},{6,2},{7,3},{8,4},{9,5},{1... | collective-permute-start | bytes 294920 | tf_op jit(solution)/shard_map/cond/branch_1_fun/ppermute | solution.py:180
  44.4 6.9 %collective-permute-start.22 = (f32[192,128]{1,0:T(8,128)S(1)}, f32[192,128]{1,0:T(8,128)S(1)}, u32[]{:S(2)}, u32[]{:S(2)}) collective-permute-start(f32[192,128]{1,0:T(8,128)S(1)} %get-tuple-element.111), channel_id=1, source_target_pairs={{0,4},{1,5},{2,6},{3,7},{4,8},{5,9},{6,10},{7,11},{8,12},{9,13},{1... | collective-permute-start | bytes 294920 | tf_op jit(solution)/shard_map/cond/branch_1_fun/ppermute | solution.py:180
  44.9 6.4 %copy-start.33 = (f32[192,128]{1,0:T(8,128)}, f32[192,128]{1,0:T(8,128)S(1)}, u32[]{:S(2)}) copy-start(f32[192,128]{1,0:T(8,128)S(1)} %collective-permute-done.17.refs_4_) | copy-start | bytes 294916 | tf_op jit(solution)/shard_map/cond
  44.9 6.4 %collective-permute-start.21 = (f32[192,128]{1,0:T(8,128)S(1)}, f32[192,128]{1,0:T(8,128)S(1)}, u32[]{:S(2)}, u32[]{:S(2)}) collective-permute-start(f32[192,128]{1,0:T(8,128)S(1)} %get-tuple-element.112), channel_id=1, source_target_pairs={{0,8},{1,9},{2,10},{3,11},{4,12},{5,13},{6,14},{7,15},{8,0},{9,1},... | collective-permute-start | bytes 294920 | tf_op jit(solution)/shard_map/cond/branch_1_fun/ppermute | solution.py:180
  46.7 4.6 %copy-start.34 = (f32[192,128]{1,0:T(8,128)}, f32[192,128]{1,0:T(8,128)S(1)}, u32[]{:S(2)}) copy-start(f32[192,128]{1,0:T(8,128)S(1)} %collective-permute-done.16.refs_3_) | copy-start | bytes 294916 | tf_op jit(solution)/shard_map/cond
  46.7 4.6 %copy-start.35 = (f32[192,128]{1,0:T(8,128)}, f32[192,128]{1,0:T(8,128)S(1)}, u32[]{:S(2)}) copy-start(f32[192,128]{1,0:T(8,128)S(1)} %collective-permute-done.15.refs_2_) | copy-start | bytes 294916 | tf_op jit(solution)/shard_map/cond
  47.5 3.9 %copy-start.36 = (f32[192,128]{1,0:T(8,128)}, f32[192,128]{1,0:T(8,128)S(1)}, u32[]{:S(2)}) copy-start(f32[192,128]{1,0:T(8,128)S(1)} %collective-permute-done.23.refs_8_) | copy-start | bytes 294916 | tf_op jit(solution)/shard_map/cond
  51.3 0.6 copy-start.37
  51.3 0.7 copy-start.38
  54.5 1.5 %collective-permute-start.48 = (f32[64,256]{1,0:T(8,128)}, f32[64,256]{1,0:T(8,128)S(1)}, u32[]{:S(2)}, u32[]{:S(2)}) collective-permute-start(f32[64,256]{1,0:T(8,128)} %param.15), channel_id=1, source_target_pairs={{0,16},{16,0},{32,48},{48,32},{64,80},{80,64},{96,112},{112,96},{1... | collective-permute-start | bytes 196616 | tf_op jit(solution)/shard_map/ppermute | solution.py:232
  56.0 19.1 %copy-start.17 = (f32[128,256]{1,0:T(8,128)}, f32[128,256]{1,0:T(8,128)S(1)}, u32[]{:S(2)}) copy-start(f32[128,256]{1,0:T(8,128)S(1)} %constant_dynamic-update-slice_fusion.pair_0) | copy-start | bytes 393220
  56.0 19.1 %collective-permute-start.51 = (f32[128,256]{1,0:T(8,128)S(1)}, f32[128,256]{1,0:T(8,128)S(1)}, u32[]{:S(2)}, u32[]{:S(2)}) collective-permute-start(f32[128,256]{1,0:T(8,128)S(1)} %constant_dynamic-update-slice_fusion.pair_0), channel_id=1, source_target_pairs={{0,96},{16,112},{32,0},{48,16},{64,32},{80,48},{96,64},{112,80},{1... | collective-permute-start | bytes 393224 | tf_op jit(solution)/shard_map/ppermute | solution.py:247
  60.8 14.3 %collective-permute-start.50 = (f32[128,256]{1,0:T(8,128)S(1)}, f32[128,256]{1,0:T(8,128)S(1)}, u32[]{:S(2)}, u32[]{:S(2)}) collective-permute-start(f32[128,256]{1,0:T(8,128)S(1)} %constant_dynamic-update-slice_fusion.pair_0), channel_id=1, source_target_pairs={{0,64},{16,80},{32,96},{48,112},{64,0},{80,16},{96,32},{112,48},{1... | collective-permute-start | bytes 393224 | tf_op jit(solution)/shard_map/ppermute | solution.py:247
  61.2 13.9 %collective-permute-start.49 = (f32[128,256]{1,0:T(8,128)S(1)}, f32[128,256]{1,0:T(8,128)S(1)}, u32[]{:S(2)}, u32[]{:S(2)}) collective-permute-start(f32[128,256]{1,0:T(8,128)S(1)} %constant_dynamic-update-slice_fusion.pair_0), channel_id=1, source_target_pairs={{0,32},{16,48},{32,64},{48,80},{64,96},{80,112},{96,0},{112,16},{1... | collective-permute-start | bytes 393224 | tf_op jit(solution)/shard_map/ppermute | solution.py:247
  75.1 0.7 copy-start.18
  75.1 0.7 copy-start.19
  75.8 0.7 copy-start.20
  78.8 11.4 %all-to-all-start.1 = ((f32[16,4,640]{2,1,0:T(4,128)}), f32[16,4,640]{2,1,0:T(4,128)S(1)}, u32[]{:S(2)}, u32[]{:S(2)}) async-start(f32[16,4,640]{2,1,0:T(4,128)} %shard_map.65), calls=%async_computation.1 | async-start | bytes 327680 | tf_op jit(solution)/shard_map/all_to_all | solution.py:261
  90.2 0.7 copy-start.16

commit v2 on v1

--- a/solution.py
+++ b/solution.py
@@ -144,14 +144,39 @@
     )(scal, acts, grads, w_in, w_out)
 
 
-def outer_kernel(tb, scal, *refs):
-    out = refs[-1]
+def fetch_all(refs, sems):
+    half = len(refs) // 2
+    copies = [pltpu.make_async_copy(refs[n], refs[half + n], sems.at[n]) for n in range(half)]
+    for copy in copies:
+        copy.start()
+    for copy in copies:
+        copy.wait()
+    return [ref[...] for ref in refs[half:]]
+
+
+def call_fetching(kernel, out_shape, scalars, operands):
+    def body(*refs):
+        first, last = len(scalars), len(scalars) + len(operands)
+        kernel(refs[:first], fetch_all(refs[first:last] + refs[last + 1 : -1], refs[-1]), refs[last])
+
+    return pl.pallas_call(
+        body,
+        in_specs=[pl.BlockSpec(memory_space=pltpu.SMEM)] * len(scalars) + [pl.BlockSpec(memory_space=pl.ANY)] * len(operands),
+        out_specs=pl.BlockSpec(memory_space=pltpu.VMEM),
+        out_shape=jax.ShapeDtypeStruct(out_shape, jnp.float32),
+        scratch_shapes=[pltpu.VMEM(v.shape, v.dtype) for v in operands] + [pltpu.SemaphoreType.DMA((len(operands),))],
+        compiler_params=pltpu.CompilerParams(vmem_limit_bytes=12 * 1024 * 1024),
+    )(*scalars, *operands)
+
+
+def outer_kernel(tb, scalars, values, out):
+    scal = scalars[0]
     row = lax.broadcasted_iota(jnp.int32, (64, 64), 0)
     col = lax.broadcasted_iota(jnp.int32, (64, 64), 1)
     order = ((row & 15) * 4 + (row >> 4) == col).astype(jnp.float32)
     each, owner = [], []
     for h in range(2):
-        a, b, c, d = (ref[...] for ref in refs[4 * h : 4 * h + 4])
+        a, b, c, d = values[4 * h : 4 * h + 4]
         rows = (a + b) + (c + d)
         product = lax.dot_general(
             rows[:, :64], rows[:, 64:], (((0,), (0,)), ((), ())),
@@ -182,32 +207,48 @@
 
 def reduce_blocks(tb, scal, acts, grads, w_in, w_out):
     x2, z2 = project(tb, (2,), scal, acts, grads, w_in, w_out)
-    got_x = [send(x2, "x", 2)]
-    got_z = [send(z2, "z", 2)]
+    from_x2, from_z2 = send(x2, "x", 2), send(z2, "z", 2)
     x1, z1, x3, z3, x0, z0 = project(tb, (1, 3, 0), scal, acts, grads, w_in, w_out)
-    got_x += [send(x1, "x", 1), send(x3, "x", 3)]
-    got_z += [send(z1, "z", 1), send(z3, "z", 3)]
-    total_x = x0 + sum(got_x)
-    total_z = z0 + sum(got_z)
+    from_x1, from_z1 = send(x1, "x", 1), send(z1, "z", 1)
+    sum_x, sum_z, x3, z3 = lax.optimization_barrier((x0 + from_x2, z0 + from_z2, x3, z3))
+    total_x = sum_x + (from_x1 + send(x3, "x", 3))
+    total_z = sum_z + (from_z1 + send(z3, "z", 3))
     final = []
     for total, axis in ((total_x, "z"), (total_z, "x")):
         final.append(total[0])
         final += [send(total[k], axis, k) for k in (2, 1, 3)]
+    return call_fetching(lambda *refs: outer_kernel(tb, *refs), (16, 4, 256), [scal], final)
+
+
+def pair_up(mine, other, _after):
+    def body(mine_ref, other_ref, _, out, sems):
+        copies = [
+            pltpu.make_async_copy(mine_ref, out.at[:64], sems.at[0]),
+            pltpu.make_async_copy(other_ref, out.at[64:], sems.at[1]),
+        ]
+        for copy in copies:
+            copy.start()
+        for copy in copies:
+            copy.wait()
+
     return pl.pallas_call(
-        lambda *refs: outer_kernel(tb, *refs),
-        in_specs=[pl.BlockSpec(memory_space=pltpu.SMEM)] + [pl.BlockSpec(memory_space=pltpu.VMEM)] * 8,
-        out_specs=pl.BlockSpec(memory_space=pltpu.VMEM),
-        out_shape=jax.ShapeDtypeStruct((16, 4, 256), jnp.float32),
-    )(scal, *final)
-
-
-def dots_kernel(received, pair_0, pair_1, pair_2, pair_3, out):
-    grads = jnp.sum(received[...], axis=0)
+        body,
+        in_specs=[pl.BlockSpec(memory_space=pl.ANY)] * 3,
+        out_specs=pl.BlockSpec(memory_space=pl.ANY),
+        out_shape=jax.ShapeDtypeStruct((128, mine.shape[1]), mine.dtype),
+        scratch_shapes=[pltpu.SemaphoreType.DMA((2,))],
+        compiler_params=pltpu.CompilerParams(vmem_limit_bytes=1024 * 1024),
+    )(mine, other, _after)
+
+
+def dots_kernel(scalars, values, out):
+    received, *pairs = values
+    grads = jnp.sum(received, axis=0)
     squares = jnp.sum(grads * grads, axis=1, keepdims=True)
     parts = []
-    for pair in (pair_0, pair_1, pair_2, pair_3):
+    for pair in pairs:
         parts.append(lax.dot_general(
-            grads, pair[...], (((1,), (1,)), ((), ())),
+            grads, pair, (((1,), (1,)), ((), ())),
             precision=lax.Precision.HIGHEST, preferred_element_type=jnp.float32,
         ))
     parts.append(jnp.broadcast_to(squares, (4, 128)))
@@ -215,8 +256,9 @@
     out[...] = jnp.broadcast_to(packed[None], out.shape)
 
 
-def scores_kernel(group, received, out):
-    sums = jnp.sum(received[...], axis=0)
+def scores_kernel(scalars, values, out):
+    group = scalars[0]
+    sums = jnp.sum(values[0], axis=0)
     scale = jnp.sqrt(sums[:, 512:640] + 1e-06)
     y, core = group[0] >> 1, group[0] & 1
     for n in range(4):
@@ -228,7 +270,6 @@
     place = lax.axis_index("units").astype(jnp.int32).reshape(1)
     group = lax.axis_index("prompts").astype(jnp.int32).reshape(1)
     smem = pl.BlockSpec(memory_space=pltpu.SMEM)
-    vmem = pl.BlockSpec(memory_space=pltpu.VMEM)
     other = lax.ppermute(val_grads, "prompts", [(n, n ^ 1) for n in range(8)])
     scal = pl.pallas_call(
         plan_kernel,
@@ -236,29 +277,20 @@
         out_specs=smem,
         out_shape=jax.ShapeDtypeStruct((8,), jnp.int32),
     )(lengths, place)
+    scal, other = lax.optimization_barrier((scal, other))
     shards = lax.switch(
         scal[6],
         [lambda *ops, tb=tb: reduce_blocks(tb, *ops) for tb in BLOCK_SIZES],
         scal, hidden_acts, out_grads, proj_in.T, proj_out.T,
     )
-    pairs = [jnp.concatenate([val_grads, other])]
+    received = lax.all_to_all(shards, "units", 0, 0, tiled=True)
+    pairs = [pair_up(val_grads, other, shards)]
     for step in (1, 3, 2):
         hops = [(2 * y + c, 2 * ((y + step) % 4) + c) for y in range(4) for c in range(2)]
         pairs.append(lax.ppermute(pairs[0], "prompts", hops))
     pairs = [pairs[0], pairs[1], pairs[3], pairs[2]]
-    received = lax.all_to_all(shards, "units", 0, 0, tiled=True)
-    packed = pl.pallas_call(
-        dots_kernel,
-        in_specs=[vmem] * 5,
-        out_specs=vmem,
-        out_shape=jax.ShapeDtypeStruct((16, 4, 640), jnp.float32),
-    )(received, *pairs)
-    return pl.pallas_call(
-        scores_kernel,
-        in_specs=[smem, vmem],
-        out_specs=vmem,
-        out_shape=jax.ShapeDtypeStruct((4, 512), jnp.float32),
-    )(group, lax.all_to_all(packed, "units", 0, 0, tiled=True))
+    packed = call_fetching(dots_kernel, (16, 4, 640), [], [received] + pairs)
+    return call_fetching(scores_kernel, (4, 512), [group], [lax.all_to_all(packed, "units", 0, 0, tiled=True)])
 
 
 def solution(mesh):

time: 93.4 us -> 84.1 us (0.900)
  local copies, waits for them, and re-layouts: 5.68 us -> 0.66 us
  Pallas kernels: 19.5 us -> 17.3 us
  waiting for transfers between devices: 18.6 us -> 17.5 us
    ppermute x12, starting transfers between devices: 24.8 us -> 22 us  [send(): return lax.ppermute(value, 'units', along(axis, step))]
    unnamed x11 -> x2, local copies, waits for them, and re-layouts: 2.84 us -> 0.01 us
    ppermute x3, starting transfers between devices: 6.17 us -> 8.37 us  [per_device(): pairs.append(lax.ppermute(pairs[0], 'prompts', hops))]
    pallas_call x2, Pallas kernels: 11.9 us -> 10.4 us  [project(): pl.pallas_call(lambda *refs: project_kernel(tb, steps, *refs), in_specs=[...]
    squeeze x2, local copies, waits for them, and re-layouts: 1.33 us -> 0.05 us  [reduce_blocks(): final += [send(total[k], axis, k) for k in (2, 1, 3)]]
    pallas_call x3 -> x4, Pallas kernels: 6.24 us -> 5.58 us  [the longest x3 5.39 us: call_fetching(): pl.pallas_call(body, in_specs=[pl.BlockSpec(memory_space=pltpu.SMEM)] * l...]
  transfers between devices with their start and end apart: 17 -> 17, of which waited for: 7 -> 7; matrix products, arithmetic and copies ran while one was open for 3% -> 0% of each run, Pallas kernels for 9% -> 10%
where the time goes in v2:
time: 84.1 us; the launch traced here: 83.5 us
  starting transfers between devices  33.9 us (40%)
  waiting for transfers between devices  17.5 us (21%)
  Pallas kernels  17.3 us (21%)
  blocking collectives  12.8 us (15%)
  between operations  0.88 us (1%)
    ppermute x12, starting transfers between devices, send(): return lax.ppermute(value, 'units', along(axis, step))  22 us
    all_to_all x1, blocking collectives, per_device(): received = lax.all_to_all(shards, 'units', 0, 0, tiled=True)  12.8 us
    pallas_call x2, Pallas kernels, project(): pl.pallas_call(lambda *refs: project_kernel(tb, steps, *refs), in_specs=[...  10.4 us
    ppermute x12, waiting for transfers between devices, send(): return lax.ppermute(value, 'units', along(axis, step))  9.42 us
    ppermute x3, starting transfers between devices, per_device(): pairs.append(lax.ppermute(pairs[0], 'prompts', hops))  8.37 us
    all_to_all x1, waiting for transfers between devices, per_device(): lax.all_to_all(packed, 'units', 0, 0, tiled=True)  7.9 us
    pallas_call x3, Pallas kernels, call_fetching(): pl.pallas_call(body, in_specs=[pl.BlockSpec(memory_space=pltpu.SMEM)] * l...  5.39 us
    all_to_all x1, starting transfers between devices, per_device(): lax.all_to_all(packed, 'units', 0, 0, tiled=True)  3.53 us
  transfers between devices with their start and end apart: 17, of which 7 were waited for; matrix products, arithmetic and copies ran while one was open for 0% of the time, Pallas kernels for 10%

profile of v2, /device:TPU:0, one launch (start us, length us, event | category | flops | bytes accessed | tf_op | source)
XLA Modules:
  0.0 83.5 jit_solution(6390092299643962697)
XLA Ops:
  0.0 0.0 collective-permute-start.48
  0.0 1.3 %shard_map.64 = s32[8]{0:T(128)S(1)} custom-call(s32[4]{0:T(128)} %lengths.1, s32[1]{0:T(128)} %bitcast.33.place), custom_call_target="tpu_custom_call" | custom-call | tf_op jit(solution)/shard_map/pallas_call | solution.py:274
  1.3 0.1 collective-permute-done.48.other_ref
  1.5 0.6 slice.99
  2.7 0.0 copy-start
  2.7 44.9 %conditional.1 = (f32[16,4,256]{2,1,0:T(4,128)S(1)}) conditional(s32[]{:T(128)} %bitcast.34, (s32[8]{0:T(128)S(1)}, bf16[4,2048,896]{2,1,0:T(8,128)(2,1)}, bf16[4,2048,256]{2,1,0:T(8,128)(2,1)}, bf16[64,896]{1,0:T(8,128)(2,1)}, bf16[64,256]{1,0:T(8,128)(2,1)}) %tuple.56, (s32[8]{0:T(128)S(1)}, ...), branch_computations={%region_0.0_spmd, %region_1.0_spmd, %region_2.0_spmd, %region_3.0_... | conditional | flops 4832624640 | bytes 124322400 | solution.py:281
  2.7 0.0 copy-start.1
  2.7 0.0 copy-start.5
  2.8 0.0 copy-start.12
  2.8 3.6 %branch_0_fun.4 = (f32[4,160,128]{2,1,0:T(8,128)S(1)}, f32[4,160,128]{2,1,0:T(8,128)S(1)}) custom-call(s32[8]{0:T(128)S(1)} %get-tuple-element.48.refs_0_, bf16[4,2048,896]{2,1,0:T(8,128)(2,1)} %get-tuple-element.50.refs_1_, bf16[4,2048,256]{2,1,0:T(8,128)(2,1)} %get-tuple-element.52.refs_2_, bf16[64,896]{1,0:T(8,128)(2,1)} %get-tuple-element.53.refs_3_, ...), custom_call_target="tpu_custom_call" | custom-call | flops 754974720 | bytes 3604480 | tf_op jit(solution)/shard_map/cond/branch_0_fun/pallas_call | solution.py:123
  6.4 3.2 %collective-permute-start = (f32[4,160,128]{2,1,0:T(8,128)S(1)}, f32[4,160,128]{2,1,0:T(8,128)S(1)}, u32[]{:S(2)}, u32[]{:S(2)}) collective-permute-start(f32[4,160,128]{2,1,0:T(8,128)S(1)} %get-tuple-element.56), channel_id=1, source_target_pairs={{0,8},{1,9},{2,10},{3,11},{4,12},{5,13},{6,14},{7,15},{8,0},{9,1},... | collective-permute-start | bytes 983048 | tf_op jit(solution)/shard_map/cond/branch_0_fun/ppermute | solution.py:205
  9.6 3.9 %collective-permute-start.1 = (f32[4,160,128]{2,1,0:T(8,128)S(1)}, f32[4,160,128]{2,1,0:T(8,128)S(1)}, u32[]{:S(2)}, u32[]{:S(2)}) collective-permute-start(f32[4,160,128]{2,1,0:T(8,128)S(1)} %get-tuple-element.58), channel_id=1, source_target_pairs={{0,2},{1,3},{2,0},{3,1},{4,6},{5,7},{6,4},{7,5},{8,10},{9,11},{10,... | collective-permute-start | bytes 983048 | tf_op jit(solution)/shard_map/cond/branch_0_fun/ppermute | solution.py:205
  13.5 6.8 %branch_0_fun.3 = (f32[4,160,128]{2,1,0:T(8,128)S(1)}, f32[4,160,128]{2,1,0:T(8,128)S(1)}, f32[4,160,128]{2,1,0:T(8,128)S(1)}, f32[4,160,128]{2,1,0:T(8,128)S(1)...) custom-call(s32[8]{0:T(128)S(1)} %get-tuple-element.48.refs_0_, bf16[4,2048,896]{2,1,0:T(8,128)(2,1)S(1)} %copy-done.1, ...), custom_call_target="tpu_custom_call" | custom-call | flops 2264924160 | bytes 10813440 | tf_op jit(solution)/shard_map/cond/branch_0_fun/pallas_call | solution.py:123
  20.3 0.7 collective-permute-start.2
  21.0 0.0 collective-permute-done
  21.0 0.4 collective-permute-done.1
  21.5 2.3 %collective-permute-start.3 = (f32[4,160,128]{2,1,0:T(8,128)S(1)}, f32[4,160,128]{2,1,0:T(8,128)S(1)}, u32[]{:S(2)}, u32[]{:S(2)}) collective-permute-start(f32[4,160,128]{2,1,0:T(8,128)S(1)} %get-tuple-element.63), channel_id=1, source_target_pairs={{0,12},{1,13},{2,14},{3,15},{4,0},{5,1},{6,2},{7,3},{8,4},{9,5},{1... | collective-permute-start | bytes 983048 | tf_op jit(solution)/shard_map/cond/branch_0_fun/ppermute | solution.py:205
  23.8 1.0 %collective-permute-start.7 = (f32[4,160,128]{2,1,0:T(8,128)S(1)}, f32[4,160,128]{2,1,0:T(8,128)S(1)}, u32[]{:S(2)}, u32[]{:S(2)}) collective-permute-start(f32[4,160,128]{2,1,0:T(8,128)S(1)} %get-tuple-element.65), channel_id=1, source_target_pairs={{0,1},{1,2},{2,3},{3,0},{4,5},{5,6},{6,7},{7,4},{8,9},{9,10},{10,1... | collective-permute-start | bytes 983048 | tf_op jit(solution)/shard_map/cond/branch_0_fun/ppermute | solution.py:205
  24.8 2.2 %collective-permute-start.8 = (f32[4,160,128]{2,1,0:T(8,128)S(1)}, f32[4,160,128]{2,1,0:T(8,128)S(1)}, u32[]{:S(2)}, u32[]{:S(2)}) collective-permute-start(f32[4,160,128]{2,1,0:T(8,128)S(1)} %get-tuple-element.66), channel_id=1, source_target_pairs={{0,3},{1,0},{2,1},{3,2},{4,7},{5,4},{6,5},{7,6},{8,11},{9,8},{10,9... | collective-permute-start | bytes 983048 | tf_op jit(solution)/shard_map/cond/branch_0_fun/ppermute | solution.py:205
  27.0 4.0 %collective-permute-done.2 = f32[4,160,128]{2,1,0:T(8,128)S(1)} collective-permute-done((f32[4,160,128]{2,1,0:T(8,128)S(1)}, f32[4,160,128]{2,1,0:T(8,128)S(1)}, u32[]{:S(2)}, u32[]{:S(2)}) %collective-permute-start.2) | collective-permute-done | bytes 327712 | tf_op jit(solution)/shard_map/cond/branch_0_fun/ppermute | solution.py:205
  31.0 0.0 collective-permute-done.3
  31.0 0.1 add_add_fusion.1
  31.1 2.9 %collective-permute-start.6 = (f32[160,128]{1,0:T(8,128)S(1)}, f32[160,128]{1,0:T(8,128)S(1)}, u32[]{:S(2)}, u32[]{:S(2)}) collective-permute-start(f32[160,128]{1,0:T(8,128)S(1)} %get-tuple-element.126), channel_id=1, source_target_pairs={{0,3},{1,0},{2,1},{3,2},{4,7},{5,4},{6,5},{7,6},{8,11},{9,8},{10,9... | collective-permute-start | bytes 245768 | tf_op jit(solution)/shard_map/cond/branch_0_fun/ppermute | solution.py:205
  34.0 0.0 collective-permute-start.5
  34.0 1.9 %collective-permute-start.4 = (f32[160,128]{1,0:T(8,128)S(1)}, f32[160,128]{1,0:T(8,128)S(1)}, u32[]{:S(2)}, u32[]{:S(2)}) collective-permute-start(f32[160,128]{1,0:T(8,128)S(1)} %get-tuple-element.128), channel_id=1, source_target_pairs={{0,2},{1,3},{2,0},{3,1},{4,6},{5,7},{6,4},{7,5},{8,10},{9,11},{10,... | collective-permute-start | bytes 245768 | tf_op jit(solution)/shard_map/cond/branch_0_fun/ppermute | solution.py:205
  35.8 0.0 collective-permute-done.7
  35.8 0.0 collective-permute-done.8
  35.9 0.1 add_add_fusion
  35.9 2.4 %collective-permute-start.11 = (f32[160,128]{1,0:T(8,128)S(1)}, f32[160,128]{1,0:T(8,128)S(1)}, u32[]{:S(2)}, u32[]{:S(2)}) collective-permute-start(f32[160,128]{1,0:T(8,128)S(1)} %get-tuple-element.122), channel_id=1, source_target_pairs={{0,12},{1,13},{2,14},{3,15},{4,0},{5,1},{6,2},{7,3},{8,4},{9,5},{1... | collective-permute-start | bytes 245768 | tf_op jit(solution)/shard_map/cond/branch_0_fun/ppermute | solution.py:205
  38.4 0.0 collective-permute-start.10
  38.4 0.0 collective-permute-done.6.refs_4_
  38.4 1.5 %collective-permute-start.9 = (f32[160,128]{1,0:T(8,128)S(1)}, f32[160,128]{1,0:T(8,128)S(1)}, u32[]{:S(2)}, u32[]{:S(2)}) collective-permute-start(f32[160,128]{1,0:T(8,128)S(1)} %get-tuple-element.124), channel_id=1, source_target_pairs={{0,8},{1,9},{2,10},{3,11},{4,12},{5,13},{6,14},{7,15},{8,0},{9,1},... | collective-permute-start | bytes 245768 | tf_op jit(solution)/shard_map/cond/branch_0_fun/ppermute | solution.py:205
  39.9 0.6 collective-permute-done.5.refs_3_
  40.5 0.0 collective-permute-done.4.refs_2_
  40.5 0.5 collective-permute-done.11.refs_8_
  41.0 3.9 %collective-permute-done.10.refs_7_ = f32[160,128]{1,0:T(8,128)S(1)} collective-permute-done((f32[160,128]{1,0:T(8,128)S(1)}, f32[160,128]{1,0:T(8,128)S(1)}, u32[]{:S(2)}, u32[]{:S(2)}) %collective-permute-start.10) | collective-permute-done | bytes 81952 | tf_op jit(solution)/shard_map/cond/branch_0_fun/ppermute | solution.py:205
  44.9 0.0 collective-permute-done.9.refs_6_
  44.9 2.5 %branch_0_fun.5 = f32[16,4,256]{2,1,0:T(4,128)S(1)} custom-call(s32[8]{0:T(128)S(1)} %get-tuple-element.48.refs_0_, f32[160,128]{1,0:T(8,128)S(1)} %get-tuple-element.129.refs_1_, f32[160,128]{1,0:T(8,128)S(1)} %collective-permute-done.4.refs_2_, f32[160,128]{1,0:T(8,128)S(1)} %collective-permute-done.5.refs_3_, ...), custom_call_target="tpu_custom_call" | custom-call | tf_op jit(solution)/shard_map/cond/branch_0_fun/pallas_call | solution.py:162
  47.6 0.2 shard_map.65.refs_1_
  47.8 7.4 %collective-permute-start.51 = (f32[128,256]{1,0:T(8,128)S(1)}, f32[128,256]{1,0:T(8,128)S(1)}, u32[]{:S(2)}, u32[]{:S(2)}) collective-permute-start(f32[128,256]{1,0:T(8,128)S(1)} %shard_map.65.refs_1_), channel_id=1, source_target_pairs={{0,96},{16,112},{32,0},{48,16},{64,32},{80,48},{96,64},{112,80},{1... | collective-permute-start | bytes 393224 | tf_op jit(solution)/shard_map/ppermute | solution.py:290
  55.2 0.0 collective-permute-start.50
  55.2 0.9 %collective-permute-start.49 = (f32[128,256]{1,0:T(8,128)S(1)}, f32[128,256]{1,0:T(8,128)S(1)}, u32[]{:S(2)}, u32[]{:S(2)}) collective-permute-start(f32[128,256]{1,0:T(8,128)S(1)} %shard_map.65.refs_1_), channel_id=1, source_target_pairs={{0,32},{16,48},{32,64},{48,80},{64,96},{80,112},{96,0},{112,16},{1... | collective-permute-start | bytes 393224 | tf_op jit(solution)/shard_map/ppermute | solution.py:290
  56.2 12.8 %all_to_all.10.refs_0_ = f32[16,4,256]{2,1,0:T(4,128)S(1)} all-to-all(f32[16,4,256]{2,1,0:T(4,128)S(1)} %get-tuple-element.154._), channel_id=1, replica_groups=mesh['prompts'=8,'units'=16] {'units'}, dimensions={0} | all-to-all | bytes 131072 | tf_op jit(solution)/shard_map/all_to_all | solution.py:286
  69.0 0.0 collective-permute-done.51.refs_4_
  69.0 2.0 %shard_map.66 = f32[16,4,640]{2,1,0:T(4,128)} custom-call(f32[16,4,256]{2,1,0:T(4,128)S(1)} %all_to_all.10.refs_0_, f32[128,256]{1,0:T(8,128)S(1)} %shard_map.65.refs_1_, f32[128,256]{1,0:T(8,128)S(1)} %collective-permute-done.49.refs_2_, f32[128,256]{1,0:T(8,128)S(1)} %collective-permute-done.50.refs_3_, f32[128,256]{1,0:T(8,128)S(1)} %collective-permute-done.51.refs_4_), custom_call_target="tpu_custom_call" | custom-call | tf_op jit(solution)/shard_map/pallas_call | solution.py:162
  71.0 3.5 %all-to-all-start.1 = ((f32[16,4,640]{2,1,0:T(4,128)}), f32[16,4,640]{2,1,0:T(4,128)S(1)}, u32[]{:S(2)}, u32[]{:S(2)}) async-start(f32[16,4,640]{2,1,0:T(4,128)} %shard_map.66), calls=%async_computation.1 | async-start | bytes 327680 | tf_op jit(solution)/shard_map/all_to_all | solution.py:293
  74.5 7.9 %all-to-all-done.1.refs_1_ = f32[16,4,640]{2,1,0:T(4,128)S(1)} async-done(((f32[16,4,640]{2,1,0:T(4,128)}), f32[16,4,640]{2,1,0:T(4,128)S(1)}, u32[]{:S(2)}, u32[]{:S(2)}) %all-to-all-start.1) | async-done | bytes 163872 | tf_op jit(solution)/shard_map/all_to_all | solution.py:293
  82.4 0.9 %shard_map.67 = f32[4,512]{1,0:T(4,128)} custom-call(s32[1]{0:T(128)} %bitcast.32.refs_0_, f32[16,4,640]{2,1,0:T(4,128)S(1)} %all-to-all-done.1.refs_1_), custom_call_target="tpu_custom_call" | custom-call | tf_op jit(solution)/shard_map/pallas_call | solution.py:162
  (10 shorter events, 0.1 us)
Async XLA Ops:
  0.0 1.5 %collective-permute-start.48 = (f32[64,256]{1,0:T(8,128)}, f32[64,256]{1,0:T(8,128)S(1)}, u32[]{:S(2)}, u32[]{:S(2)}) collective-permute-start(f32[64,256]{1,0:T(8,128)} %mine_ref.1), channel_id=1, source_target_pairs={{0,16},{16,0},{32,48},{48,32},{64,80},{80,64},{96,112},{112,96},{1... | collective-permute-start | bytes 196616 | tf_op jit(solution)/shard_map/ppermute | solution.py:273
  2.7 44.9 %copy-start = (f32[64,256]{1,0:T(8,128)S(1)}, f32[64,256]{1,0:T(8,128)}, u32[]{:S(2)}) copy-start(f32[64,256]{1,0:T(8,128)} %mine_ref.1) | copy-start | bytes 196612
  2.7 10.8 %copy-start.1 = (bf16[4,2048,896]{2,1,0:T(8,128)(2,1)S(1)}, bf16[4,2048,896]{2,1,0:T(8,128)(2,1)}, u32[]{:S(2)}) copy-start(bf16[4,2048,896]{2,1,0:T(8,128)(2,1)} %get-tuple-element.50.refs_1_) | copy-start | bytes 44040196 | tf_op jit(solution)/shard_map/cond
  2.7 10.8 %copy-start.5 = (bf16[4,2048,256]{2,1,0:T(8,128)(2,1)S(1)}, bf16[4,2048,256]{2,1,0:T(8,128)(2,1)}, u32[]{:S(2)}) copy-start(bf16[4,2048,256]{2,1,0:T(8,128)(2,1)} %get-tuple-element.52.refs_2_) | copy-start | bytes 12582916 | tf_op jit(solution)/shard_map/cond
  2.8 10.7 %copy-start.12 = (bf16[64,256]{1,0:T(8,128)(2,1)S(1)}, bf16[64,256]{1,0:T(8,128)(2,1)}, u32[]{:S(2)}) copy-start(bf16[64,256]{1,0:T(8,128)(2,1)} %get-tuple-element.54.refs_4_) | copy-start | bytes 98308 | tf_op jit(solution)/shard_map/cond
  6.4 14.6 %collective-permute-start = (f32[4,160,128]{2,1,0:T(8,128)S(1)}, f32[4,160,128]{2,1,0:T(8,128)S(1)}, u32[]{:S(2)}, u32[]{:S(2)}) collective-permute-start(f32[4,160,128]{2,1,0:T(8,128)S(1)} %get-tuple-element.56), channel_id=1, source_target_pairs={{0,8},{1,9},{2,10},{3,11},{4,12},{5,13},{6,14},{7,15},{8,0},{9,1},... | collective-permute-start | bytes 983048 | tf_op jit(solution)/shard_map/cond/branch_0_fun/ppermute | solution.py:205
  9.6 11.8 %collective-permute-start.1 = (f32[4,160,128]{2,1,0:T(8,128)S(1)}, f32[4,160,128]{2,1,0:T(8,128)S(1)}, u32[]{:S(2)}, u32[]{:S(2)}) collective-permute-start(f32[4,160,128]{2,1,0:T(8,128)S(1)} %get-tuple-element.58), channel_id=1, source_target_pairs={{0,2},{1,3},{2,0},{3,1},{4,6},{5,7},{6,4},{7,5},{8,10},{9,11},{10,... | collective-permute-start | bytes 983048 | tf_op jit(solution)/shard_map/cond/branch_0_fun/ppermute | solution.py:205
  20.3 10.7 %collective-permute-start.2 = (f32[4,160,128]{2,1,0:T(8,128)S(1)}, f32[4,160,128]{2,1,0:T(8,128)S(1)}, u32[]{:S(2)}, u32[]{:S(2)}) collective-permute-start(f32[4,160,128]{2,1,0:T(8,128)S(1)} %get-tuple-element.62), channel_id=1, source_target_pairs={{0,4},{1,5},{2,6},{3,7},{4,8},{5,9},{6,10},{7,11},{8,12},{9,13},{1... | collective-permute-start | bytes 983048 | tf_op jit(solution)/shard_map/cond/branch_0_fun/ppermute | solution.py:205
  21.5 9.5 %collective-permute-start.3 = (f32[4,160,128]{2,1,0:T(8,128)S(1)}, f32[4,160,128]{2,1,0:T(8,128)S(1)}, u32[]{:S(2)}, u32[]{:S(2)}) collective-permute-start(f32[4,160,128]{2,1,0:T(8,128)S(1)} %get-tuple-element.63), channel_id=1, source_target_pairs={{0,12},{1,13},{2,14},{3,15},{4,0},{5,1},{6,2},{7,3},{8,4},{9,5},{1... | collective-permute-start | bytes 983048 | tf_op jit(solution)/shard_map/cond/branch_0_fun/ppermute | solution.py:205
  23.8 12.1 %collective-permute-start.7 = (f32[4,160,128]{2,1,0:T(8,128)S(1)}, f32[4,160,128]{2,1,0:T(8,128)S(1)}, u32[]{:S(2)}, u32[]{:S(2)}) collective-permute-start(f32[4,160,128]{2,1,0:T(8,128)S(1)} %get-tuple-element.65), channel_id=1, source_target_pairs={{0,1},{1,2},{2,3},{3,0},{4,5},{5,6},{6,7},{7,4},{8,9},{9,10},{10,1... | collective-permute-start | bytes 983048 | tf_op jit(solution)/shard_map/cond/branch_0_fun/ppermute | solution.py:205
  24.8 11.1 %collective-permute-start.8 = (f32[4,160,128]{2,1,0:T(8,128)S(1)}, f32[4,160,128]{2,1,0:T(8,128)S(1)}, u32[]{:S(2)}, u32[]{:S(2)}) collective-permute-start(f32[4,160,128]{2,1,0:T(8,128)S(1)} %get-tuple-element.66), channel_id=1, source_target_pairs={{0,3},{1,0},{2,1},{3,2},{4,7},{5,4},{6,5},{7,6},{8,11},{9,8},{10,9... | collective-permute-start | bytes 983048 | tf_op jit(solution)/shard_map/cond/branch_0_fun/ppermute | solution.py:205
  31.1 7.3 %collective-permute-start.6 = (f32[160,128]{1,0:T(8,128)S(1)}, f32[160,128]{1,0:T(8,128)S(1)}, u32[]{:S(2)}, u32[]{:S(2)}) collective-permute-start(f32[160,128]{1,0:T(8,128)S(1)} %get-tuple-element.126), channel_id=1, source_target_pairs={{0,3},{1,0},{2,1},{3,2},{4,7},{5,4},{6,5},{7,6},{8,11},{9,8},{10,9... | collective-permute-start | bytes 245768 | tf_op jit(solution)/shard_map/cond/branch_0_fun/ppermute | solution.py:205
  34.0 6.5 %collective-permute-start.5 = (f32[160,128]{1,0:T(8,128)S(1)}, f32[160,128]{1,0:T(8,128)S(1)}, u32[]{:S(2)}, u32[]{:S(2)}) collective-permute-start(f32[160,128]{1,0:T(8,128)S(1)} %get-tuple-element.127), channel_id=1, source_target_pairs={{0,1},{1,2},{2,3},{3,0},{4,5},{5,6},{6,7},{7,4},{8,9},{9,10},{10,1... | collective-permute-start | bytes 245768 | tf_op jit(solution)/shard_map/cond/branch_0_fun/ppermute | solution.py:205
  34.0 6.5 %collective-permute-start.4 = (f32[160,128]{1,0:T(8,128)S(1)}, f32[160,128]{1,0:T(8,128)S(1)}, u32[]{:S(2)}, u32[]{:S(2)}) collective-permute-start(f32[160,128]{1,0:T(8,128)S(1)} %get-tuple-element.128), channel_id=1, source_target_pairs={{0,2},{1,3},{2,0},{3,1},{4,6},{5,7},{6,4},{7,5},{8,10},{9,11},{10,... | collective-permute-start | bytes 245768 | tf_op jit(solution)/shard_map/cond/branch_0_fun/ppermute | solution.py:205
  35.9 5.1 %collective-permute-start.11 = (f32[160,128]{1,0:T(8,128)S(1)}, f32[160,128]{1,0:T(8,128)S(1)}, u32[]{:S(2)}, u32[]{:S(2)}) collective-permute-start(f32[160,128]{1,0:T(8,128)S(1)} %get-tuple-element.122), channel_id=1, source_target_pairs={{0,12},{1,13},{2,14},{3,15},{4,0},{5,1},{6,2},{7,3},{8,4},{9,5},{1... | collective-permute-start | bytes 245768 | tf_op jit(solution)/shard_map/cond/branch_0_fun/ppermute | solution.py:205
  38.4 6.5 %collective-permute-start.10 = (f32[160,128]{1,0:T(8,128)S(1)}, f32[160,128]{1,0:T(8,128)S(1)}, u32[]{:S(2)}, u32[]{:S(2)}) collective-permute-start(f32[160,128]{1,0:T(8,128)S(1)} %get-tuple-element.123), channel_id=1, source_target_pairs={{0,4},{1,5},{2,6},{3,7},{4,8},{5,9},{6,10},{7,11},{8,12},{9,13},{1... | collective-permute-start | bytes 245768 | tf_op jit(solution)/shard_map/cond/branch_0_fun/ppermute | solution.py:205
  38.4 6.5 %collective-permute-start.9 = (f32[160,128]{1,0:T(8,128)S(1)}, f32[160,128]{1,0:T(8,128)S(1)}, u32[]{:S(2)}, u32[]{:S(2)}) collective-permute-start(f32[160,128]{1,0:T(8,128)S(1)} %get-tuple-element.124), channel_id=1, source_target_pairs={{0,8},{1,9},{2,10},{3,11},{4,12},{5,13},{6,14},{7,15},{8,0},{9,1},... | collective-permute-start | bytes 245768 | tf_op jit(solution)/shard_map/cond/branch_0_fun/ppermute | solution.py:205
  47.8 21.1 %collective-permute-start.51 = (f32[128,256]{1,0:T(8,128)S(1)}, f32[128,256]{1,0:T(8,128)S(1)}, u32[]{:S(2)}, u32[]{:S(2)}) collective-permute-start(f32[128,256]{1,0:T(8,128)S(1)} %shard_map.65.refs_1_), channel_id=1, source_target_pairs={{0,96},{16,112},{32,0},{48,16},{64,32},{80,48},{96,64},{112,80},{1... | collective-permute-start | bytes 393224 | tf_op jit(solution)/shard_map/ppermute | solution.py:290
  55.2 13.7 %collective-permute-start.50 = (f32[128,256]{1,0:T(8,128)S(1)}, f32[128,256]{1,0:T(8,128)S(1)}, u32[]{:S(2)}, u32[]{:S(2)}) collective-permute-start(f32[128,256]{1,0:T(8,128)S(1)} %shard_map.65.refs_1_), channel_id=1, source_target_pairs={{0,64},{16,80},{32,96},{48,112},{64,0},{80,16},{96,32},{112,48},{1... | collective-permute-start | bytes 393224 | tf_op jit(solution)/shard_map/ppermute | solution.py:290
  55.2 13.7 %collective-permute-start.49 = (f32[128,256]{1,0:T(8,128)S(1)}, f32[128,256]{1,0:T(8,128)S(1)}, u32[]{:S(2)}, u32[]{:S(2)}) collective-permute-start(f32[128,256]{1,0:T(8,128)S(1)} %shard_map.65.refs_1_), channel_id=1, source_target_pairs={{0,32},{16,48},{32,64},{48,80},{64,96},{80,112},{96,0},{112,16},{1... | collective-permute-start | bytes 393224 | tf_op jit(solution)/shard_map/ppermute | solution.py:290
  71.0 11.4 %all-to-all-start.1 = ((f32[16,4,640]{2,1,0:T(4,128)}), f32[16,4,640]{2,1,0:T(4,128)S(1)}, u32[]{:S(2)}, u32[]{:S(2)}) async-start(f32[16,4,640]{2,1,0:T(4,128)} %shard_map.66), calls=%async_computation.1 | async-start | bytes 327680 | tf_op jit(solution)/shard_map/all_to_all | solution.py:293
